TPU v7x, 512 devices: a whole 4x8x8 slice. The times are simulated.
512 devices in a mesh: slab: 64 (over z_hi, y, core), dp: 8 (over z_lo, x).
Axes of the slice: x: 4, y: 8, z: 8 (z_hi: 4, z_lo: 2; z = z_hi * 2 + z_lo), core: 2. Of those that a mesh axis runs over, the one named last changes fastest.
Arguments:
- universe: bfloat16 [8, 4, 256, 4, 512], P('dp', None, 'slab'), may hold values from -6 to 6
- cotangent: bfloat16 [8, 64, 64, 1, 128], P('dp', None, 'slab'), may hold values from -0.15625 to 0.15625
- conv1_weight: bfloat16 [32, 108], replicated, may hold values from -0.625 to 0.625
- conv1_bias: float32 [32], replicated, may hold values from -3 to 3
- conv2_weight: bfloat16 [64, 864], replicated, may hold values from -0.21875 to 0.21875
- conv2_bias: float32 [64], replicated, may hold values from -3 to 3
- owners: int32 [460, 1], replicated, may hold values from 0 to 7; in each aligned block of 460 rows (0 to 459, 460 to 919, ...) at most 138 rows name the same one
- accumulated: float32 [1104, 128], P('dp'), may hold values from -1 to 1
Outputs:
- features: bfloat16 [8, 64, 64, 1, 128], P('dp', None, 'slab')
- owned: float32 [1104, 128], P('dp')
Inputs may be any that keep to these rules, and one draw needn't show every extreme that they name: `owners`: each index of dp owns at most 138 blocks, exactly 138 for one of them, and at least one for each.
All inputs are finite; a program needn't handle non-finite values.
Results may differ from a plain program's by a relative error of at most 0.0014.
The roundings to bfloat16 on the way count: a program that leaves them out, or rounds other values in their place, can miss the bound.
Values may be sent and summed in bfloat16 or wider, within the bound.
No kernel may reach another device: no remote copies, remote signals or barrier semaphores. Data moves between devices by JAX's collectives and lax.ppermute only.
A program may use at most 64 MiB of HBM per device.

v0:
```python
import jax
import jax.numpy as jnp
from jax import lax
from jax.sharding import PartitionSpec as P

NB = 460
SLOPE = 0.3
OFFSETS = [
    (first, second, third) for first in range(3) for second in range(3) for third in range(3)
]


def with_halo(block, sides, width):
    for axis, dim in sides:
        count = lax.axis_size(axis)
        forward = [(i, i + 1) for i in range(count - 1)]
        forward.append((count - 1, 0))
        backward = [(target, source) for source, target in forward]
        low = lax.ppermute(
            lax.slice_in_dim(block, block.shape[dim] - width, None, axis=dim), axis, forward
        )
        high = lax.ppermute(lax.slice_in_dim(block, 0, width, axis=dim), axis, backward)
        block = jnp.concatenate([low, block, high], axis=dim)
    return block


def pad_sides(field):
    return jnp.pad(field, ((0, 0), (0, 0), (1, 1), (1, 1)))


def tap_stack(padded, deep_rows, high_rows, wide_rows, flipped):
    pieces = [
        padded[:, first : first + deep_rows, second : second + high_rows, third : third + wide_rows]
        for first, second, third in OFFSETS
    ]
    if flipped:
        pieces = pieces[::-1]
    stacked = jnp.stack(pieces, axis=0)
    return stacked.reshape(27 * padded.shape[0], deep_rows * high_rows * wide_rows)


def average(field):
    chans, deep_rows, high_rows, wide_rows = field.shape
    return field.reshape(chans, deep_rows // 2, 2, high_rows // 2, 2, wide_rows // 2, 2).mean(
        axis=(2, 4, 6)
    )


def spread_back(field):
    return jnp.repeat(jnp.repeat(jnp.repeat(field, 2, axis=1), 2, axis=2), 2, axis=3) * 0.125


def leaky_relu(value):
    return jnp.where(value > 0, value, SLOPE * value)


def slope_mask(value):
    return jnp.where(value > 0, 1.0, SLOPE)


def place_blocks(owners, blocks, ranks, capacity):
    owner_of = owners[:, 0]
    member = (owner_of[:, None] == jnp.arange(ranks, dtype=jnp.int32)[None, :]).astype(jnp.int32)
    before = jnp.cumsum(member, axis=0) - member
    slot_index = jnp.sum(before * member, axis=1)
    target = owner_of * capacity + slot_index
    placing = (jnp.arange(ranks * capacity, dtype=jnp.int32)[:, None] == target[None, :]).astype(
        jnp.float32
    )
    return jnp.dot(placing, blocks, precision=lax.Precision.HIGHEST)


def body(
    universe, cotangent, conv1_weight, conv1_bias, conv2_weight, conv2_bias, owners, accumulated
):
    field = universe[0]
    chans_in, deep_rows, high_rows, wide_rows = field.shape
    chan_one = conv1_weight.shape[0]
    chan_two = conv2_weight.shape[0]
    half_deep, half_high, half_wide = (deep_rows // 2, high_rows // 2, wide_rows // 2)
    extended = with_halo(field, (("slab", 1),), 1)
    cols_one = tap_stack(pad_sides(extended), deep_rows, high_rows, wide_rows, False)
    pre_one = (
        jnp.dot(conv1_weight, cols_one, preferred_element_type=jnp.float32) + conv1_bias[:, None]
    )
    pre_one = pre_one.reshape(chan_one, deep_rows, high_rows, wide_rows)
    pooled = average(leaky_relu(pre_one)).astype(jnp.bfloat16)
    rimmed = with_halo(pooled, (("slab", 1),), 1)
    cols_two = tap_stack(pad_sides(rimmed), half_deep, half_high, half_wide, False)
    pre_two = (
        jnp.dot(conv2_weight, cols_two, preferred_element_type=jnp.float32) + conv2_bias[:, None]
    )
    pre_two = pre_two.reshape(chan_two, half_deep, half_high, half_wide)
    feature = average(leaky_relu(pre_two)).astype(jnp.bfloat16)
    delta_two = (spread_back(cotangent[0].astype(jnp.float32)) * slope_mask(pre_two)).astype(
        jnp.bfloat16
    )
    flat_two = delta_two.reshape(chan_two, -1)
    grad_w2 = jnp.einsum("oc,kc->ok", flat_two, cols_two, preferred_element_type=jnp.float32)
    grad_b2 = jnp.sum(flat_two.astype(jnp.float32), axis=1)
    delta_rim = with_halo(delta_two, (("slab", 1),), 1)
    cols_back = tap_stack(pad_sides(delta_rim), half_deep, half_high, half_wide, True)
    weight_back = (
        conv2_weight.reshape(chan_two, 27, chan_one)
        .transpose(2, 1, 0)
        .reshape(chan_one, 27 * chan_two)
    )
    back_pooled = jnp.dot(weight_back, cols_back, preferred_element_type=jnp.float32)
    back_pooled = back_pooled.reshape(chan_one, half_deep, half_high, half_wide)
    delta_one = (spread_back(back_pooled) * slope_mask(pre_one)).astype(jnp.bfloat16)
    flat_one = delta_one.reshape(chan_one, -1)
    grad_w1 = jnp.einsum("oc,kc->ok", flat_one, cols_one, preferred_element_type=jnp.float32)
    grad_b1 = jnp.sum(flat_one.astype(jnp.float32), axis=1)
    vector = jnp.concatenate([grad_w1.reshape(-1), grad_b1, grad_w2.reshape(-1), grad_b2])
    blocks = jnp.pad(vector, (0, NB * 128 - vector.shape[0])).reshape(NB, 128)
    ranks = lax.axis_size("dp")
    capacity = accumulated.shape[0]
    totals = lax.psum(blocks, "slab")
    packed = place_blocks(owners, totals, ranks, capacity)
    mine = lax.psum_scatter(packed, "dp", scatter_dimension=0, tiled=True)
    owned = accumulated + mine
    return (feature[None], owned)


def solution(mesh):
    in_specs = (
        P("dp", None, "slab", None, None),
        P("dp", None, "slab", None, None),
        P(),
        P(),
        P(),
        P(),
        P(),
        P("dp", None),
    )
    out_specs = (P("dp", None, "slab", None, None), P("dp", None))
    return jax.shard_map(body, mesh=mesh, in_specs=in_specs, out_specs=out_specs, check_vma=False)
```

profile of v0, /device:TPU:64, one launch (start us, length us, event | category | flops | bytes accessed | tf_op | source)
XLA Modules:
  0.0 733.3 jit_solution(869186729282681174)
XLA Ops:
  8.0 1.9 collective-permute-start
  9.9 12.4 %collective-permute-start.1 = (bf16[4,1,4,512]{3,2,1,0:T(4,128)(2,1)S(1)}, bf16[4,1,4,512]{3,2,1,0:T(4,128)(2,1)S(1)}, u32[]{:S(2)}, u32[]{:S(2)}) collective-permute-start(bf16[4,1,4,512]{3,2,1,0:T(4,128)(2,1)S(1)} %get-tuple-element.22), channel_id=1, source_target_pairs={{8,0},{16,8},{24,16},{32,24},{40,32},{48,40},{56,48},{64,56},{72,6... | collective-permute-start | bytes 49160 | tf_op jit(solution)/shard_map/ppermute | solution.py:22
  23.7 1.1 reduce-window.6
  25.2 1.0 select_maximum_fusion.4
  29.0 1.4 constant_dynamic-update-slice_fusion.22
  36.0 1.5 constant_dynamic-update-slice_fusion.13
  43.1 1.4 constant_dynamic-update-slice_fusion.4
  47.4 3.8 reshape.172
  51.7 2.6 copy.90
  54.3 6.5 fusion.2
  62.3 1.9 collective-permute-start.2
  64.2 8.0 %collective-permute-start.3 = (bf16[32,1,2,256]{0,3,2,1:T(8,128)(2,1)}, bf16[32,1,2,256]{0,3,2,1:T(8,128)(2,1)}, u32[]{:S(2)}, u32[]{:S(2)}) collective-permute-start(bf16[32,1,2,256]{0,3,2,1:T(8,128)(2,1)} %get-tuple-element.18), channel_id=1, source_target_pairs={{8,0},{16,8},{24,16},{32,24},{40,32},{48,40},{56,48},{64,56},{72,6... | collective-permute-start | bytes 98312 | tf_op jit(solution)/shard_map/ppermute | solution.py:22
  72.4 0.9 broadcast_in_dim.46
  73.3 1.2 copy.101
  75.3 1.6 copy.94
  76.9 1.7 copy.96
  78.6 1.7 copy.97
  80.3 1.9 reshape.180
  82.2 1.2 select_maximum_fusion
  86.4 1.7 fusion.43
  90.3 0.8 fusion.38
  98.7 0.8 fusion.28
  101.0 1.7 fusion.25
  105.7 8.2 %copy.91 = bf16[27,32,2,2,256]{4,3,2,1,0:T(2,128)(2,1)} copy(bf16[27,32,2,2,256]{1,4,3,2,0:T(8,128)(2,1)} %fusion.20) | data formatting | bytes 3538944 | tf_op jit(solution)/shard_map/stack | solution.py:38
  113.9 5.2 reshape.174
  119.1 3.3 convert_reduce_fusion.1
  122.6 1.0 multiply_convert_fusion.4
  124.3 1.9 collective-permute-start.4
  126.3 7.9 %collective-permute-start.5 = (bf16[64,1,2,256]{3,2,1,0:T(2,128)(2,1)}, bf16[64,1,2,256]{3,2,1,0:T(2,128)(2,1)}, u32[]{:S(2)}, u32[]{:S(2)}) collective-permute-start(bf16[64,1,2,256]{3,2,1,0:T(2,128)(2,1)} %get-tuple-element.20), channel_id=1, source_target_pairs={{8,0},{16,8},{24,16},{32,24},{40,32},{48,40},{56,48},{64,56},{72,6... | collective-permute-start | bytes 196616 | tf_op jit(solution)/shard_map/ppermute | solution.py:22
  134.1 2.9 fusion.62
  137.3 1.8 reshape.182
  139.1 2.6 select_maximum_fusion.2
  141.7 1.0 constant_dynamic-update-slice_fusion.53
  142.7 1.0 constant_dynamic-update-slice_fusion.52
  144.4 1.0 constant_dynamic-update-slice_fusion.50
  145.4 1.6 constant_dynamic-update-slice_fusion.49
  147.8 0.9 constant_dynamic-update-slice_fusion.47
  148.6 0.9 constant_dynamic-update-slice_fusion.46
  150.3 1.0 constant_dynamic-update-slice_fusion.44
  151.2 1.0 constant_dynamic-update-slice_fusion.43
  152.2 0.8 constant_dynamic-update-slice_fusion.42
  153.0 1.0 constant_dynamic-update-slice_fusion.41
  154.8 0.8 constant_dynamic-update-slice_fusion.39
  155.5 0.9 constant_dynamic-update-slice_fusion.38
  156.4 0.9 constant_dynamic-update-slice_fusion.37
  158.1 1.0 constant_dynamic-update-slice_fusion.35
  159.0 1.0 constant_dynamic-update-slice_fusion.34
  160.0 0.8 constant_dynamic-update-slice_fusion.33
  160.8 1.0 constant_dynamic-update-slice_fusion.32
  161.8 1.6 constant_dynamic-update-slice_fusion.31
  164.2 0.9 constant_dynamic-update-slice_fusion.29
  165.0 0.9 constant_dynamic-update-slice_fusion.28
  166.6 8.9 %reshape.178 = bf16[1728,1024]{1,0:T(8,128)(2,1)} reshape(bf16[27,64,2,2,256]{4,3,2,1,0:T(2,128)(2,1)} %constant_dynamic-update-slice_fusion.27) | data formatting | bytes 7077888 | tf_op jit(solution)/shard_map/reshape | solution.py:39
  175.6 2.7 fusion.11
  178.8 3.4 broadcast_in_dim.44
  182.2 3.6 copy.99
  185.9 1.6 convert_reduce_fusion
  188.4 1.6 concatenate.39
  190.7 1.3 dynamic-slice.4
  193.3 498.6 %all-reduce.9.cloned.1.call-done = f32[460,128]{1,0:T(8,128)} async-done(((f32[460,128]{1,0:T(8,128)}), f32[460,128]{1,0:T(8,128)}) %all-reduce.9.cloned.1.call-update) | async-done | bytes 235536 | tf_op jit(solution)/shard_map/psum | solution.py:118
  691.9 2.1 fusion.3
  694.0 23.7 %fusion = f32[144,128]{1,0:T(8,128)S(1)} fusion(f32[1104,128]{1,0:T(8,128)S(1)} %fusion.3), kind=kCustom, calls=%all-reduce-scatter | all-reduce-scatter fusion | flops 147457 | bytes 641024
  717.7 1.9 collective-permute-start.6
  720.3 5.2 collective-permute-done.6
  (119 shorter events, 50.5 us)
Async XLA Ops:
  7.2 44.1 %copy-start = (bf16[32,108]{1,0:T(8,128)(2,1)S(1)}, bf16[32,108]{1,0:T(8,128)(2,1)}, u32[]{:S(2)}) copy-start(bf16[32,108]{1,0:T(8,128)(2,1)} %param.10) | copy-start | bytes 20740
  7.2 684.7 %all-reduce.9.cloned.1.call-start = ((), (), s32[]{:S(2)}) async-start(), calls=%async_computation | async-start | bytes 475136 | tf_op jit(solution)/shard_map/psum | solution.py:118
  8.0 17.2 %collective-permute-start = (bf16[4,1,4,512]{3,2,1,0:T(4,128)(2,1)S(1)}, bf16[4,1,4,512]{3,2,1,0:T(4,128)(2,1)S(1)}, u32[]{:S(2)}, u32[]{:S(2)}) collective-permute-start(bf16[4,1,4,512]{3,2,1,0:T(4,128)(2,1)S(1)} %get-tuple-element.21), channel_id=1, source_target_pairs={{0,8},{8,16},{16,24},{24,32},{32,40},{40,48},{48,56},{56,64},{64,7... | collective-permute-start | bytes 49160 | tf_op jit(solution)/shard_map/ppermute | solution.py:19
  9.9 15.3 %collective-permute-start.1 = (bf16[4,1,4,512]{3,2,1,0:T(4,128)(2,1)S(1)}, bf16[4,1,4,512]{3,2,1,0:T(4,128)(2,1)S(1)}, u32[]{:S(2)}, u32[]{:S(2)}) collective-permute-start(bf16[4,1,4,512]{3,2,1,0:T(4,128)(2,1)S(1)} %get-tuple-element.22), channel_id=1, source_target_pairs={{8,0},{16,8},{24,16},{32,24},{40,32},{48,40},{56,48},{64,56},{72,6... | collective-permute-start | bytes 49160 | tf_op jit(solution)/shard_map/ppermute | solution.py:22
  26.9 24.4 %copy-start.11 = (f32[32]{0:T(128)S(1)}, f32[32]{0:T(128)}, u32[]{:S(2)}) copy-start(f32[32]{0:T(128)} %param.11) | copy-start | bytes 388
  54.3 18.0 %copy-start.9 = (s32[460,1]{0,1:T(1,128)S(1)}, s32[460,1]{0,1:T(1,128)}, u32[]{:S(2)}) copy-start(s32[460,1]{0,1:T(1,128)} %param.14) | copy-start | bytes 5524
  60.7 0.8 copy-start.1
  62.3 19.8 %collective-permute-start.2 = (bf16[32,1,2,256]{0,3,2,1:T(8,128)(2,1)}, bf16[32,1,2,256]{0,3,2,1:T(8,128)(2,1)}, u32[]{:S(2)}, u32[]{:S(2)}) collective-permute-start(bf16[32,1,2,256]{0,3,2,1:T(8,128)(2,1)} %get-tuple-element.17), channel_id=1, source_target_pairs={{0,8},{8,16},{16,24},{24,32},{32,40},{40,48},{48,56},{56,64},{64,7... | collective-permute-start | bytes 98312 | tf_op jit(solution)/shard_map/ppermute | solution.py:19
  64.2 17.9 %collective-permute-start.3 = (bf16[32,1,2,256]{0,3,2,1:T(8,128)(2,1)}, bf16[32,1,2,256]{0,3,2,1:T(8,128)(2,1)}, u32[]{:S(2)}, u32[]{:S(2)}) collective-permute-start(bf16[32,1,2,256]{0,3,2,1:T(8,128)(2,1)} %get-tuple-element.18), channel_id=1, source_target_pairs={{8,0},{16,8},{24,16},{32,24},{40,32},{48,40},{56,48},{64,56},{72,6... | collective-permute-start | bytes 98312 | tf_op jit(solution)/shard_map/ppermute | solution.py:22
  83.4 10.8 %copy-start.2 = (f32[32,2,2,256]{0,3,2,1:T(8,128)S(1)}, f32[32,2,2,256]{0,3,2,1:T(8,128)}, u32[]{:S(2)}) copy-start(f32[32,2,2,256]{0,3,2,1:T(8,128)} %copy-done.1) | copy-start | bytes 393220
  113.9 5.2 copy-start.6
  113.9 5.2 copy-start.12
  124.3 14.8 %collective-permute-start.4 = (bf16[64,1,2,256]{3,2,1,0:T(2,128)(2,1)}, bf16[64,1,2,256]{3,2,1,0:T(2,128)(2,1)}, u32[]{:S(2)}, u32[]{:S(2)}) collective-permute-start(bf16[64,1,2,256]{3,2,1,0:T(2,128)(2,1)} %get-tuple-element.19), channel_id=1, source_target_pairs={{0,8},{8,16},{16,24},{24,32},{32,40},{40,48},{48,56},{56,64},{64,7... | collective-permute-start | bytes 196616 | tf_op jit(solution)/shard_map/ppermute | solution.py:19
  126.3 12.8 %collective-permute-start.5 = (bf16[64,1,2,256]{3,2,1,0:T(2,128)(2,1)}, bf16[64,1,2,256]{3,2,1,0:T(2,128)(2,1)}, u32[]{:S(2)}, u32[]{:S(2)}) collective-permute-start(bf16[64,1,2,256]{3,2,1,0:T(2,128)(2,1)} %get-tuple-element.20), channel_id=1, source_target_pairs={{8,0},{16,8},{24,16},{32,24},{40,32},{48,40},{56,48},{64,56},{72,6... | collective-permute-start | bytes 196616 | tf_op jit(solution)/shard_map/ppermute | solution.py:22
  137.2 16.7 %copy-start.5 = (f32[64,256]{1,0:T(8,128)S(1)}, f32[64,256]{1,0:T(8,128)}, u32[]{:S(2)}) copy-start(f32[64,256]{1,0:T(8,128)} %copy.94) | copy-start | bytes 196612
  166.6 8.9 %copy-start.7 = (bf16[32,1728]{1,0:T(8,128)(2,1)S(1)}, bf16[32,1728]{1,0:T(8,128)(2,1)}, u32[]{:S(2)}) copy-start(bf16[32,1728]{1,0:T(8,128)(2,1)} %reshape.180) | copy-start | bytes 331780
  185.9 2.5 copy-start.4
  185.9 2.5 copy-start.10
  185.9 6.7 copy-start.3
  187.5 538.3 %copy-start.8 = (f32[138,128]{1,0:T(8,128)S(1)}, f32[138,128]{1,0:T(8,128)}, u32[]{:S(2)}) copy-start(f32[138,128]{1,0:T(8,128)} %param.15) | copy-start | bytes 211972
  717.7 7.8 %collective-permute-start.6 = (f32[42,128]{1,0:T(8,128)S(1)}, f32[42,128]{1,0:T(8,128)S(1)}, u32[]{:S(2)}, u32[]{:S(2)}) collective-permute-start(f32[42,128]{1,0:T(8,128)S(1)} %slice.446), channel_id=1, source_target_pairs={{0,1},{1,2},{2,3},{3,4},{4,5},{5,6},{6,7},{8,9},{9,10},{10,11},{11... | collective-permute-start | bytes 64520
Sparse Core Ops, SparseCore 0:
  190.8 501.0 all-reduce.8
where the time goes:
time: 735 us; the launch traced here: 733 us
  waiting for transfers between devices  504 us (69%)
  local copies, waits for them, and re-layouts  114 us (16%)
  starting transfers between devices  36 us (5%)
  other arithmetic  28.8 us (4%)
  blocking collectives  23.7 us (3%)
  between operations  15.1 us (2%)
  matrix products  12.1 us (2%)
    psum x1, waiting for transfers between devices, body(): totals = lax.psum(blocks, 'slab')  499 us
    unnamed x101, local copies, waits for them, and re-layouts  60 us
    ppermute x3, starting transfers between devices, with_halo(): lax.ppermute(lax.slice_in_dim(block, 0, width, axis=dim), axis, backward)  28.3 us
    unnamed x1, blocking collectives  23.7 us
    reshape x3, local copies, waits for them, and re-layouts, tap_stack(): stacked.reshape(27 * padded.shape[0], deep_rows * high_rows * wide_rows)  17.9 us
  transfers between devices with their start and end apart: 8, of which 2 were waited for; matrix products, arithmetic and copies ran while one was open for 3% of the time, Pallas kernels for 0%

commit v1 on v0

--- a/solution.py
+++ b/solution.py
@@ -8,6 +8,11 @@
 OFFSETS = [
     (first, second, third) for first in range(3) for second in range(3) for third in range(3)
 ]
+
+
+def summed_here(value, axis):
+    parts = lax.all_gather(value, axis)
+    return jnp.sum(parts, axis=0)
 
 
 def with_halo(block, sides, width):
@@ -115,7 +120,7 @@
     blocks = jnp.pad(vector, (0, NB * 128 - vector.shape[0])).reshape(NB, 128)
     ranks = lax.axis_size("dp")
     capacity = accumulated.shape[0]
-    totals = lax.psum(blocks, "slab")
+    totals = summed_here(blocks, "slab")
     packed = place_blocks(owners, totals, ranks, capacity)
     mine = lax.psum_scatter(packed, "dp", scatter_dimension=0, tiled=True)
     owned = accumulated + mine

time: 735 us -> 364 us (0.50)
  waiting for transfers between devices: 504 us -> 129 us
    psum x1 -> x0, waiting for transfers between devices: 499 us -> none  [body(): totals = lax.psum(blocks, 'slab')]
    all_gather x0 -> x1, waiting for transfers between devices: none -> 124 us  [summed_here(): parts = lax.all_gather(value, axis)]
  transfers between devices with their start and end apart: 8 -> 8, of which waited for: 2 -> 3; matrix products, arithmetic and copies ran while one was open for 3% -> 5% of each run, Pallas kernels for 0% -> 0%
where the time goes in v1:
time: 364 us; the launch traced here: 363 us
  waiting for transfers between devices  129 us (35%)
  local copies, waits for them, and re-layouts  114 us (31%)
  starting transfers between devices  37.5 us (10%)
  other arithmetic  33.4 us (9%)
  blocking collectives  23.1 us (6%)
  between operations  15.1 us (4%)
  matrix products  10.7 us (3%)
    all_gather x1, waiting for transfers between devices, summed_here(): parts = lax.all_gather(value, axis)  124 us
    unnamed x101, local copies, waits for them, and re-layouts  60 us
    ppermute x3, starting transfers between devices, with_halo(): lax.ppermute(lax.slice_in_dim(block, 0, width, axis=dim), axis, backward)  28.3 us
    unnamed x1, blocking collectives  23.1 us
    reshape x3, local copies, waits for them, and re-layouts, tap_stack(): stacked.reshape(27 * padded.shape[0], deep_rows * high_rows * wide_rows)  17.9 us
    unnamed x8, other arithmetic  11 us
    another operation x4, local copies, waits for them, and re-layouts, tap_stack(): stacked = jnp.stack(pieces, axis=0)  10.5 us
  transfers between devices with their start and end apart: 8, of which 3 were waited for; matrix products, arithmetic and copies ran while one was open for 5% of the time, Pallas kernels for 0%

profile of v1, /device:TPU:64, one launch (start us, length us, event | category | flops | bytes accessed | tf_op | source)
XLA Modules:
  0.0 362.8 jit_solution(7889948540648993306)
XLA Ops:
  8.0 1.9 collective-permute-start
  9.9 12.4 %collective-permute-start.1 = (bf16[4,1,4,512]{3,2,1,0:T(4,128)(2,1)S(1)}, bf16[4,1,4,512]{3,2,1,0:T(4,128)(2,1)S(1)}, u32[]{:S(2)}, u32[]{:S(2)}) collective-permute-start(bf16[4,1,4,512]{3,2,1,0:T(4,128)(2,1)S(1)} %get-tuple-element.22), channel_id=1, source_target_pairs={{8,0},{16,8},{24,16},{32,24},{40,32},{48,40},{56,48},{64,56},{72,6... | collective-permute-start | bytes 49160 | tf_op jit(solution)/shard_map/ppermute | solution.py:27
  22.3 1.4 collective-permute-done.1
  23.7 1.0 select_maximum_fusion.4
  27.5 1.4 constant_dynamic-update-slice_fusion.22
  34.5 1.5 constant_dynamic-update-slice_fusion.13
  41.6 1.4 constant_dynamic-update-slice_fusion.4
  45.9 3.8 %reshape.169 = bf16[108,8192]{1,0:T(8,128)(2,1)S(1)} reshape(bf16[27,4,4,4,512]{4,3,2,1,0:T(4,128)(2,1)} %constant_dynamic-update-slice_fusion) | data formatting | bytes 3538944 | tf_op jit(solution)/shard_map/reshape | solution.py:44
  50.2 2.6 copy.90
  52.8 6.5 %fusion.2 = f32[32,2,2,256]{0,3,2,1:T(8,128)S(1)} fusion(f32[32,2,2,2,2,256,2]{0,6,5,4,3,2,1:T(2,128)} %bitcast.360), kind=kLoop, calls=%fused_computation.3 | loop fusion | flops 1015808 | bytes 1179648 | tf_op jit(solution)/shard_map/reduce_sum | solution.py:49
  60.8 1.9 collective-permute-start.2
  62.7 8.0 %collective-permute-start.3 = (bf16[32,1,2,256]{0,3,2,1:T(8,128)(2,1)}, bf16[32,1,2,256]{0,3,2,1:T(8,128)(2,1)}, u32[]{:S(2)}, u32[]{:S(2)}) collective-permute-start(bf16[32,1,2,256]{0,3,2,1:T(8,128)(2,1)} %get-tuple-element.18), channel_id=1, source_target_pairs={{8,0},{16,8},{24,16},{32,24},{40,32},{48,40},{56,48},{64,56},{72,6... | collective-permute-start | bytes 98312 | tf_op jit(solution)/shard_map/ppermute | solution.py:27
  70.9 0.9 broadcast_in_dim.46
  71.8 1.2 copy.101
  73.7 1.6 copy.94
  75.4 1.7 copy.96
  77.1 1.7 copy.97
  78.8 1.9 reshape.177
  80.7 1.2 select_maximum_fusion
  84.9 1.7 fusion.43
  88.8 0.8 fusion.38
  97.2 0.8 fusion.28
  99.5 1.7 fusion.25
  104.2 8.2 %copy.91 = bf16[27,32,2,2,256]{4,3,2,1,0:T(2,128)(2,1)} copy(bf16[27,32,2,2,256]{1,4,3,2,0:T(8,128)(2,1)} %fusion.20) | data formatting | bytes 3538944 | tf_op jit(solution)/shard_map/stack | solution.py:43
  112.4 5.2 %reshape.171 = bf16[864,1024]{1,0:T(8,128)(2,1)} reshape(bf16[27,32,2,2,256]{4,3,2,1,0:T(2,128)(2,1)} %copy.91) | data formatting | bytes 3538944 | tf_op jit(solution)/shard_map/reshape | solution.py:44
  117.6 2.8 convert_reduce_fusion.1
  120.6 1.0 multiply_convert_fusion.4
  122.3 1.9 collective-permute-start.4
  124.3 7.9 %collective-permute-start.5 = (bf16[64,1,2,256]{3,2,1,0:T(2,128)(2,1)}, bf16[64,1,2,256]{3,2,1,0:T(2,128)(2,1)}, u32[]{:S(2)}, u32[]{:S(2)}) collective-permute-start(bf16[64,1,2,256]{3,2,1,0:T(2,128)(2,1)} %get-tuple-element.20), channel_id=1, source_target_pairs={{8,0},{16,8},{24,16},{32,24},{40,32},{48,40},{56,48},{64,56},{72,6... | collective-permute-start | bytes 196616 | tf_op jit(solution)/shard_map/ppermute | solution.py:27
  132.1 2.9 fusion.62
  135.3 1.8 reshape.179
  137.1 2.6 select_maximum_fusion.2
  139.7 1.0 constant_dynamic-update-slice_fusion.53
  140.7 1.0 constant_dynamic-update-slice_fusion.52
  142.4 1.0 constant_dynamic-update-slice_fusion.50
  143.4 1.6 constant_dynamic-update-slice_fusion.49
  145.8 0.9 constant_dynamic-update-slice_fusion.47
  146.7 0.9 constant_dynamic-update-slice_fusion.46
  148.3 1.0 constant_dynamic-update-slice_fusion.44
  149.3 1.0 constant_dynamic-update-slice_fusion.43
  151.0 1.0 constant_dynamic-update-slice_fusion.41
  152.8 0.8 constant_dynamic-update-slice_fusion.39
  153.6 0.9 constant_dynamic-update-slice_fusion.38
  154.4 0.9 constant_dynamic-update-slice_fusion.37
  156.1 1.0 constant_dynamic-update-slice_fusion.35
  157.0 1.0 constant_dynamic-update-slice_fusion.34
  158.8 1.0 constant_dynamic-update-slice_fusion.32
  159.8 1.6 constant_dynamic-update-slice_fusion.31
  162.2 0.9 constant_dynamic-update-slice_fusion.29
  163.1 0.9 constant_dynamic-update-slice_fusion.28
  164.7 8.9 %reshape.175 = bf16[1728,1024]{1,0:T(8,128)(2,1)} reshape(bf16[27,64,2,2,256]{4,3,2,1,0:T(2,128)(2,1)} %constant_dynamic-update-slice_fusion.27) | data formatting | bytes 7077888 | tf_op jit(solution)/shard_map/reshape | solution.py:44
  173.6 2.7 fusion.11
  176.9 3.4 broadcast_in_dim.44
  180.3 3.6 copy.99
  183.9 1.6 convert_reduce_fusion
  186.4 1.6 concatenate.39
  188.7 1.1 reduce-window.6
  190.1 1.3 dynamic-slice.4
  192.9 123.9 %all-gather.2.cloned.1.call-done = f32[64,460,128]{2,1,0:T(8,128)} async-done(((f32[1,460,128]{2,1,0:T(8,128)}), f32[64,460,128]{2,1,0:T(8,128)}) %all-gather.2.cloned.1.call-update) | async-done | bytes 15073296 | tf_op jit(solution)/shard_map/all_gather | solution.py:14
  316.8 6.0 %reduce_sum.59 = f32[460,128]{1,0:T(8,128)S(1)} reduce(f32[64,460,128]{2,1,0:T(8,128)} %all-gather.2.cloned.1.call-done, f32[]{:T(128)} %constant.9.clone.1), dimensions={0}, to_apply=%region_7.8 | reduce | flops 3709440 | bytes 15308804 | tf_op jit(solution)/shard_map/reduce_sum | solution.py:15
  322.9 1.2 fusion.3
  324.0 23.1 %fusion = f32[144,128]{1,0:T(8,128)S(1)} fusion(f32[1104,128]{1,0:T(8,128)S(1)} %fusion.3), kind=kCustom, calls=%all-reduce-scatter | all-reduce-scatter fusion | flops 147457 | bytes 641024
  347.2 3.5 collective-permute-start.6
  351.4 3.6 %collective-permute-done.6 = f32[42,128]{1,0:T(8,128)S(1)} collective-permute-done((f32[42,128]{1,0:T(8,128)S(1)}, f32[42,128]{1,0:T(8,128)S(1)}, u32[]{:S(2)}, u32[]{:S(2)}) %collective-permute-start.6) | collective-permute-done | bytes 21536
  (120 shorter events, 50.7 us)
Async XLA Ops:
  7.2 42.6 %copy-start = (bf16[32,108]{1,0:T(8,128)(2,1)S(1)}, bf16[32,108]{1,0:T(8,128)(2,1)}, u32[]{:S(2)}) copy-start(bf16[32,108]{1,0:T(8,128)(2,1)} %param.10) | copy-start | bytes 20740
  7.2 309.7 %all-gather.2.cloned.1.call-start = ((), (), s32[]{:S(2)}) async-start(), calls=%async_computation | async-start | bytes 15441920 | tf_op jit(solution)/shard_map/all_gather | solution.py:14
  8.0 14.3 %collective-permute-start = (bf16[4,1,4,512]{3,2,1,0:T(4,128)(2,1)S(1)}, bf16[4,1,4,512]{3,2,1,0:T(4,128)(2,1)S(1)}, u32[]{:S(2)}, u32[]{:S(2)}) collective-permute-start(bf16[4,1,4,512]{3,2,1,0:T(4,128)(2,1)S(1)} %get-tuple-element.21), channel_id=1, source_target_pairs={{0,8},{8,16},{16,24},{24,32},{32,40},{40,48},{48,56},{56,64},{64,7... | collective-permute-start | bytes 49160 | tf_op jit(solution)/shard_map/ppermute | solution.py:24
  9.9 13.8 %collective-permute-start.1 = (bf16[4,1,4,512]{3,2,1,0:T(4,128)(2,1)S(1)}, bf16[4,1,4,512]{3,2,1,0:T(4,128)(2,1)S(1)}, u32[]{:S(2)}, u32[]{:S(2)}) collective-permute-start(bf16[4,1,4,512]{3,2,1,0:T(4,128)(2,1)S(1)} %get-tuple-element.22), channel_id=1, source_target_pairs={{8,0},{16,8},{24,16},{32,24},{40,32},{48,40},{56,48},{64,56},{72,6... | collective-permute-start | bytes 49160 | tf_op jit(solution)/shard_map/ppermute | solution.py:27
  25.4 24.4 %copy-start.11 = (f32[32]{0:T(128)S(1)}, f32[32]{0:T(128)}, u32[]{:S(2)}) copy-start(f32[32]{0:T(128)} %param.11) | copy-start | bytes 388
  52.8 18.0 %copy-start.10 = (bf16[1,64,1,1,128]{4,1,3,2,0:T(8,128)(2,1)S(1)}, bf16[1,64,1,1,128]{4,1,3,2,0:T(8,128)(2,1)}, u32[]{:S(2)}) copy-start(bf16[1,64,1,1,128]{4,1,3,2,0:T(8,128)(2,1)} %param.9) | copy-start | bytes 49156
  59.2 0.8 copy-start.1
  60.8 19.8 %collective-permute-start.2 = (bf16[32,1,2,256]{0,3,2,1:T(8,128)(2,1)}, bf16[32,1,2,256]{0,3,2,1:T(8,128)(2,1)}, u32[]{:S(2)}, u32[]{:S(2)}) collective-permute-start(bf16[32,1,2,256]{0,3,2,1:T(8,128)(2,1)} %get-tuple-element.17), channel_id=1, source_target_pairs={{0,8},{8,16},{16,24},{24,32},{32,40},{40,48},{48,56},{56,64},{64,7... | collective-permute-start | bytes 98312 | tf_op jit(solution)/shard_map/ppermute | solution.py:24
  62.7 17.9 %collective-permute-start.3 = (bf16[32,1,2,256]{0,3,2,1:T(8,128)(2,1)}, bf16[32,1,2,256]{0,3,2,1:T(8,128)(2,1)}, u32[]{:S(2)}, u32[]{:S(2)}) collective-permute-start(bf16[32,1,2,256]{0,3,2,1:T(8,128)(2,1)} %get-tuple-element.18), channel_id=1, source_target_pairs={{8,0},{16,8},{24,16},{32,24},{40,32},{48,40},{56,48},{64,56},{72,6... | collective-permute-start | bytes 98312 | tf_op jit(solution)/shard_map/ppermute | solution.py:27
  81.9 10.8 %copy-start.2 = (f32[32,2,2,256]{0,3,2,1:T(8,128)S(1)}, f32[32,2,2,256]{0,3,2,1:T(8,128)}, u32[]{:S(2)}) copy-start(f32[32,2,2,256]{0,3,2,1:T(8,128)} %copy-done.1) | copy-start | bytes 393220
  112.4 5.2 %copy-start.6 = (bf16[64,864]{1,0:T(8,128)(2,1)S(1)}, bf16[64,864]{1,0:T(8,128)(2,1)}, u32[]{:S(2)}) copy-start(bf16[64,864]{1,0:T(8,128)(2,1)} %param.12) | copy-start | bytes 331780
  112.4 5.2 %copy-start.12 = (f32[64]{0:T(128)S(1)}, f32[64]{0:T(128)}, u32[]{:S(2)}) copy-start(f32[64]{0:T(128)} %param.13) | copy-start | bytes 772
  122.3 14.8 %collective-permute-start.4 = (bf16[64,1,2,256]{3,2,1,0:T(2,128)(2,1)}, bf16[64,1,2,256]{3,2,1,0:T(2,128)(2,1)}, u32[]{:S(2)}, u32[]{:S(2)}) collective-permute-start(bf16[64,1,2,256]{3,2,1,0:T(2,128)(2,1)} %get-tuple-element.19), channel_id=1, source_target_pairs={{0,8},{8,16},{16,24},{24,32},{32,40},{40,48},{48,56},{56,64},{64,7... | collective-permute-start | bytes 196616 | tf_op jit(solution)/shard_map/ppermute | solution.py:24
  124.3 12.9 %collective-permute-start.5 = (bf16[64,1,2,256]{3,2,1,0:T(2,128)(2,1)}, bf16[64,1,2,256]{3,2,1,0:T(2,128)(2,1)}, u32[]{:S(2)}, u32[]{:S(2)}) collective-permute-start(bf16[64,1,2,256]{3,2,1,0:T(2,128)(2,1)} %get-tuple-element.20), channel_id=1, source_target_pairs={{8,0},{16,8},{24,16},{32,24},{40,32},{48,40},{56,48},{64,56},{72,6... | collective-permute-start | bytes 196616 | tf_op jit(solution)/shard_map/ppermute | solution.py:27
  135.2 16.8 %copy-start.5 = (f32[64,256]{1,0:T(8,128)S(1)}, f32[64,256]{1,0:T(8,128)}, u32[]{:S(2)}) copy-start(f32[64,256]{1,0:T(8,128)} %copy.94) | copy-start | bytes 196612
  164.7 8.9 %copy-start.7 = (bf16[32,1728]{1,0:T(8,128)(2,1)S(1)}, bf16[32,1728]{1,0:T(8,128)(2,1)}, u32[]{:S(2)}) copy-start(bf16[32,1728]{1,0:T(8,128)(2,1)} %reshape.177) | copy-start | bytes 331780
  183.9 2.5 copy-start.4
  183.9 4.8 %copy-start.9 = (s32[460,1]{0,1:T(1,128)S(1)}, s32[460,1]{0,1:T(1,128)}, u32[]{:S(2)}) copy-start(s32[460,1]{0,1:T(1,128)} %param.14) | copy-start | bytes 5524
  183.9 8.3 %copy-start.3 = (f32[64,1024]{1,0:T(8,128)S(1)}, f32[64,1024]{1,0:T(8,128)}, u32[]{:S(2)}) copy-start(f32[64,1024]{1,0:T(8,128)} %get-tuple-element.23) | copy-start | bytes 786436
  192.9 162.4 %copy-start.8 = (f32[138,128]{1,0:T(8,128)S(1)}, f32[138,128]{1,0:T(8,128)}, u32[]{:S(2)}) copy-start(f32[138,128]{1,0:T(8,128)} %param.15) | copy-start | bytes 211972
  347.2 7.8 %collective-permute-start.6 = (f32[42,128]{1,0:T(8,128)S(1)}, f32[42,128]{1,0:T(8,128)S(1)}, u32[]{:S(2)}, u32[]{:S(2)}) collective-permute-start(f32[42,128]{1,0:T(8,128)S(1)} %slice.446), channel_id=1, source_target_pairs={{0,1},{1,2},{2,3},{3,4},{4,5},{5,6},{6,7},{8,9},{9,10},{10,11},{11... | collective-permute-start | bytes 64520
Sparse Core Ops, SparseCore 0:
  188.8 128.0 all-gather.1
